TPU v7x, 128 devices: a whole 4x4x4 slice. The times are simulated.
128 devices in a mesh: seq: 8 (over x_hi, z), res: 16 (over x_lo, y, core).
Axes of the slice: x: 4 (x_hi: 2, x_lo: 2; x = x_hi * 2 + x_lo), y: 4, z: 4, core: 2. Of those that a mesh axis runs over, the one named last changes fastest.
Arguments:
- alignment: bfloat16 [32, 768, 768], P('seq', 'res'), may hold values from -6 to 6
- cotangent: bfloat16 [32, 768, 768], P('seq', 'res'), may hold values from -6 to 6
- gain_row: float32 [768], replicated, may hold values from 0.25 to 1.75
- query_row: bfloat16 [768, 768], replicated, may hold values from -0.25 to 0.25
- key_row: bfloat16 [768, 768], replicated, may hold values from -1.2 to 1.2
- value_row: bfloat16 [768, 768], replicated, may hold values from -0.21875 to 0.21875
- out_row: bfloat16 [768, 768], replicated, may hold values from -0.21875 to 0.21875
- gain_col: float32 [768], replicated, may hold values from 0.25 to 1.75
- query_col: bfloat16 [768, 768], replicated, may hold values from -0.25 to 0.25
- key_col: bfloat16 [768, 768], replicated, may hold values from -3.6 to 3.6
- value_col: bfloat16 [768, 768], replicated, may hold values from -0.21875 to 0.21875
- out_col: bfloat16 [768, 768], replicated, may hold values from -0.21875 to 0.21875
Outputs:
- block_out: bfloat16 [32, 768, 768], P('seq', 'res')
- input_grad: bfloat16 [32, 768, 768], P('seq', 'res')
All inputs are finite; a program needn't handle non-finite values.
Results may differ from a plain program's by a relative error of at most 0.02.
Values may be sent and summed in bfloat16 or wider, within the bound.
No kernel may reach another device: no remote copies, remote signals or barrier semaphores. Data moves between devices by JAX's collectives and lax.ppermute only.
A program may use at most 192 MiB of HBM per device.

v0:
```python
import math

import jax
import jax.numpy as jnp
from jax import lax
from jax.sharding import PartitionSpec as P

HEADS = 12
HEAD_DIM = 64


def normalize(values, gain):
    mean = jnp.mean(values, axis=-1, keepdims=True)
    centred = values - mean
    spread = jnp.mean(centred * centred, axis=-1, keepdims=True)
    return centred * lax.rsqrt(spread + 1e-05) * gain


def project(flat, weight):
    return jnp.dot(flat, weight, preferred_element_type=jnp.float32)


def back_project(flat, weight):
    return jnp.dot(flat, weight.T, preferred_element_type=jnp.float32)


def softmax_grad(probs, grads, scale):
    return probs * (grads - jnp.sum(probs * grads, axis=-1, keepdims=True)) * scale


def local(
    alignment,
    cotangent,
    gain_row,
    query_row,
    key_row,
    value_row,
    out_row,
    gain_col,
    query_col,
    key_col,
    value_col,
    out_col,
):
    f32 = jnp.float32
    bf16 = jnp.bfloat16
    seq_rows, res_cols, model_width = alignment.shape
    tokens = seq_rows * res_cols
    total_seqs = seq_rows * lax.axis_size("seq")
    shape_heads = (seq_rows, res_cols, HEADS, HEAD_DIM)
    row_scale = 1.0 / math.sqrt(HEAD_DIM * total_seqs)
    col_scale = 1.0 / math.sqrt(HEAD_DIM)
    flat_input = alignment.astype(f32).reshape(tokens, model_width)
    normed = normalize(flat_input, gain_row).astype(bf16)
    row_query = project(normed, query_row).astype(bf16).reshape(shape_heads)
    row_key = project(normed, key_row).astype(bf16).reshape(shape_heads)
    row_value = project(normed, value_row).astype(bf16).reshape(shape_heads)
    key_all, value_all = (
        lax.all_gather(row_key, "res", axis=1, tiled=True),
        lax.all_gather(row_value, "res", axis=1, tiled=True),
    )
    partial_logits = jnp.einsum("sihd,sjhd->hij", row_query, key_all, preferred_element_type=f32)
    row_logits = (
        lax.psum(partial_logits.astype(jnp.bfloat16), "seq").astype(jnp.float32) * row_scale
    )
    row_probs = jax.nn.softmax(row_logits, axis=-1)
    row_weights = row_probs.astype(bf16)
    row_att = jnp.einsum(
        "hij,sjhd->sihd", row_weights, value_all, preferred_element_type=f32
    ).astype(bf16)
    middle = (flat_input + project(row_att.reshape(tokens, model_width), out_row)).astype(bf16)
    middle_f = middle.astype(f32)
    normed_col = normalize(middle_f, gain_col).astype(bf16)
    col_query = project(normed_col, query_col).astype(bf16).reshape(seq_rows, res_cols, model_width)
    col_key = project(normed_col, key_col).astype(bf16).reshape(seq_rows, res_cols, model_width)
    col_value = project(normed_col, value_col).astype(bf16).reshape(seq_rows, res_cols, model_width)
    whole_query, whole_key, whole_value = (
        lax.all_to_all(col_query, "seq", split_axis=1, concat_axis=0, tiled=True),
        lax.all_to_all(col_key, "seq", split_axis=1, concat_axis=0, tiled=True),
        lax.all_to_all(col_value, "seq", split_axis=1, concat_axis=0, tiled=True),
    )
    all_seqs, few_cols = (whole_query.shape[0], whole_query.shape[1])
    col_heads = (all_seqs, few_cols, HEADS, HEAD_DIM)
    whole_query = whole_query.reshape(col_heads)
    whole_key = whole_key.reshape(col_heads)
    whole_value = whole_value.reshape(col_heads)
    col_logits = (
        jnp.einsum("schd,tchd->chst", whole_query, whole_key, preferred_element_type=f32)
        * col_scale
    )
    col_probs = jax.nn.softmax(col_logits, axis=-1)
    col_weights = col_probs.astype(bf16)
    col_att = jnp.einsum(
        "chst,tchd->schd", col_weights, whole_value, preferred_element_type=f32
    ).astype(bf16)
    col_back = lax.all_to_all(
        col_att.reshape(all_seqs, few_cols, model_width),
        "seq",
        split_axis=0,
        concat_axis=1,
        tiled=True,
    )
    block_out = (middle_f + project(col_back.reshape(tokens, model_width), out_col)).astype(bf16)
    grad_out = cotangent.reshape(tokens, model_width)
    grad_col_att = (
        back_project(grad_out, out_col).astype(bf16).reshape(seq_rows, res_cols, model_width)
    )
    grad_whole = lax.all_to_all(
        grad_col_att, "seq", split_axis=1, concat_axis=0, tiled=True
    ).reshape(col_heads)
    col_grad_probs = jnp.einsum(
        "schd,tchd->chst", grad_whole, whole_value, preferred_element_type=f32
    )
    col_dlogits = softmax_grad(col_probs, col_grad_probs, col_scale).astype(bf16)
    grad_col_q = jnp.einsum(
        "chst,tchd->schd", col_dlogits, whole_key, preferred_element_type=f32
    ).astype(bf16)
    grad_col_k = jnp.einsum(
        "chst,schd->tchd", col_dlogits, whole_query, preferred_element_type=f32
    ).astype(bf16)
    grad_col_v = jnp.einsum(
        "chst,schd->tchd", col_weights, grad_whole, preferred_element_type=f32
    ).astype(bf16)
    flat_shape = (all_seqs, few_cols, model_width)
    grad_q_back, grad_k_back, grad_v_back = (
        lax.all_to_all(
            grad_col_q.reshape(flat_shape), "seq", split_axis=0, concat_axis=1, tiled=True
        ),
        lax.all_to_all(
            grad_col_k.reshape(flat_shape), "seq", split_axis=0, concat_axis=1, tiled=True
        ),
        lax.all_to_all(
            grad_col_v.reshape(flat_shape), "seq", split_axis=0, concat_axis=1, tiled=True
        ),
    )
    grad_normed_col = (
        back_project(grad_q_back.reshape(tokens, model_width), query_col)
        + back_project(grad_k_back.reshape(tokens, model_width), key_col)
        + back_project(grad_v_back.reshape(tokens, model_width), value_col)
    )
    _, pull_col = jax.vjp(lambda values: normalize(values, gain_col), middle_f)
    grad_middle = (grad_out.astype(f32) + pull_col(grad_normed_col)[0]).astype(bf16)
    grad_row_att = back_project(grad_middle, out_row).astype(bf16).reshape(shape_heads)
    partial_grads = jnp.einsum(
        "sihd,sjhd->hij", grad_row_att, value_all, preferred_element_type=f32
    )
    grad_full = lax.psum(partial_grads.astype(jnp.bfloat16), "seq").astype(jnp.float32)
    row_dlogits = softmax_grad(row_probs, grad_full, row_scale).astype(bf16)
    grad_row_q = jnp.einsum(
        "hij,sjhd->sihd", row_dlogits, key_all, preferred_element_type=f32
    ).astype(bf16)
    key_terms = jnp.einsum("hij,sihd->sjhd", row_dlogits, row_query, preferred_element_type=f32)
    value_terms = jnp.einsum(
        "hij,sihd->sjhd", row_weights, grad_row_att, preferred_element_type=f32
    )
    key_summed, value_summed = (
        lax.psum_scatter(
            key_terms.astype(jnp.bfloat16), "res", scatter_dimension=1, tiled=True
        ).astype(jnp.float32),
        lax.psum_scatter(
            value_terms.astype(jnp.bfloat16), "res", scatter_dimension=1, tiled=True
        ).astype(jnp.float32),
    )
    grad_row_k = key_summed.astype(bf16)
    grad_row_v = value_summed.astype(bf16)
    grad_normed = (
        back_project(grad_row_q.reshape(tokens, model_width), query_row)
        + back_project(grad_row_k.reshape(tokens, model_width), key_row)
        + back_project(grad_row_v.reshape(tokens, model_width), value_row)
    )
    _, pull_row = jax.vjp(lambda values: normalize(values, gain_row), flat_input)
    input_grad = (grad_middle.astype(f32) + pull_row(grad_normed)[0]).astype(bf16)
    return (
        block_out.reshape(seq_rows, res_cols, model_width),
        input_grad.reshape(seq_rows, res_cols, model_width),
    )


def solution(mesh):
    return jax.shard_map(
        local,
        mesh=mesh,
        in_specs=(
            P("seq", "res", None),
            P("seq", "res", None),
            P(),
            P(),
            P(),
            P(),
            P(),
            P(),
            P(),
            P(),
            P(),
            P(),
        ),
        out_specs=(P("seq", "res", None), P("seq", "res", None)),
        check_vma=False,
    )
```

profile of v0, /device:TPU:1, one launch (start us, length us, event | category | flops | bytes accessed | tf_op | source)
XLA Modules:
  0.0 704.1 jit_solution(7977434795596280375)
XLA Ops:
  19.0 57.8 %all-gather.5.cloned.1.call-done = bf16[4,768,12,64]{3,1,0,2:T(8,128)(2,1)} async-done(((bf16[4,48,12,64]{3,1,0,2:T(8,128)(2,1)}), bf16[4,768,12,64]{3,1,0,2:T(8,128)(2,1)}) %all-gather.5.cloned.1.call-update) | async-done | bytes 4718608 | tf_op jit(solution)/shard_map/all_gather | solution.py:59
  76.8 7.5 %bitcast_convert_fusion.1 = bf16[12,48,768]{2,1,0:T(8,128)(2,1)} fusion(bf16[4,768,12,64]{3,1,0,2:T(8,128)(2,1)} %all-gather.5.cloned.1.call-done, bf16[4,48,12,64]{3,2,1,0:T(8,128)(2,1)S(1)} %reshape.173), kind=kOutput, calls=%fused_computation.12 | convolution fusion | flops 226934784 | bytes 5898240 | tf_op jit(solution)/shard_map/sihd,sjhd->hij/dot_general | solution.py:62
  88.2 6.6 all-to-all-start.4
  94.7 73.1 %all-reduce.7.cloned.1.call-done = bf16[12,48,768]{2,1,0:T(8,128)(2,1)} async-done(((bf16[12,48,768]{2,1,0:T(8,128)(2,1)}), bf16[12,48,768]{2,1,0:T(8,128)(2,1)}) %all-reduce.7.cloned.1.call-update) | async-done | bytes 884752 | tf_op jit(solution)/shard_map/psum | solution.py:64
  167.8 3.1 fusion.77
  171.0 59.1 %all-gather.3.cloned.1.call-done = bf16[4,768,12,64]{3,1,0,2:T(8,128)(2,1)} async-done(((bf16[4,48,12,64]{3,1,0,2:T(8,128)(2,1)}), bf16[4,768,12,64]{3,1,0,2:T(8,128)(2,1)}) %all-gather.3.cloned.1.call-update) | async-done | bytes 4718608 | tf_op jit(solution)/shard_map/all_gather | solution.py:60
  230.1 6.1 fusion.21
  243.5 6.6 all-to-all-start
  252.7 5.2 all-to-all-done
  257.9 4.2 all-to-all-start.2
  264.7 5.4 all-to-all-done.2
  270.0 4.2 all-to-all-start.1
  275.1 2.4 reshape.187
  284.8 3.0 fusion.79
  287.8 2.8 fusion.44
  290.6 4.0 fusion.18
  296.9 2.4 reshape.204
  299.3 6.4 all-to-all-start.5
  305.7 4.1 fusion.19
  314.3 6.6 all-to-all-start.6
  329.3 6.7 all-to-all-start.7
  339.8 2.7 fusion.84
  352.6 7.6 %bitcast_convert_fusion = bf16[12,48,768]{2,1,0:T(8,128)(2,1)} fusion(bf16[4,768,12,64]{3,1,0,2:T(8,128)(2,1)} %all-gather.3.cloned.1.call-done, bf16[4,48,12,64]{3,2,1,0:T(8,128)(2,1)S(1)} %reshape.194), kind=kOutput, calls=%fused_computation.11 | convolution fusion | flops 226934784 | bytes 5898240 | tf_op jit(solution)/shard_map/sihd,sjhd->hij/dot_general | solution.py:144
  360.2 5.2 convert_bitcast_fusion
  365.4 15.4 %copy.98 = bf16[4,768,12,64]{3,0,2,1:T(4,128)(2,1)} copy(bf16[4,768,12,64]{1,3,0,2:T(8,128)(2,1)} %convert_bitcast_fusion) | data formatting | bytes 9437184 | tf_op jit(solution)/shard_map/convert_element_type | solution.py:161
  380.8 65.3 %all-reduce.9.cloned.1.call-done = bf16[12,48,768]{2,1,0:T(8,128)(2,1)} async-done(((bf16[12,48,768]{2,1,0:T(8,128)(2,1)}), bf16[12,48,768]{2,1,0:T(8,128)(2,1)}) %all-reduce.9.cloned.1.call-update) | async-done | bytes 884752 | tf_op jit(solution)/shard_map/psum | solution.py:147
  446.1 7.1 %convert_bitcast_fusion.1 = bf16[4,768,12,64]{1,3,0,2:T(8,128)(2,1)} fusion(bf16[12,48,768]{2,1,0:T(8,128)(2,1)} %all-reduce.9.cloned.1.call-done, bf16[4,48,12,64]{3,2,1,0:T(8,128)(2,1)S(1)} %copy-done.14, f32[12,48,768]{2,1,0:T(8,128)} %get-tuple-element.9, f32[12,48]{1,0:T(8,128)S(1)} %copy-done.31), kind=kOutput, calls=%fused_computation.5 | convolution fusion | flops 232834368 | bytes 7670016 | tf_op jit(solution)/shard_map/hij,sihd->sjhd/dot_general | solution.py:152
  453.2 15.4 %copy.95 = bf16[4,768,12,64]{3,0,2,1:T(4,128)(2,1)} copy(bf16[4,768,12,64]{1,3,0,2:T(8,128)(2,1)} %convert_bitcast_fusion.1) | data formatting | bytes 9437184 | tf_op jit(solution)/shard_map/convert_element_type | solution.py:158
  472.9 3.8 all-to-all-start.3
  478.0 6.6 all-to-all-done.3
  485.8 8.4 %fusion.22 = bf16[4,48,12,64]{3,1,0,2:T(8,128)(2,1)S(1)} fusion(bf16[4,768,12,64]{3,1,0,2:T(8,128)(2,1)} %all-gather.5.cloned.1.call-done, bf16[12,48,768]{2,1,0:T(8,128)(2,1)} %all-reduce.9.cloned.1.call-done, f32[12,48,768]{2,1,0:T(8,128)} %get-tuple-element.9, f32[12,48]{1,0:T(8,128)S(1)} %copy-done.31), kind=kOutput, calls=%fused_computation.43 | convolution fusion | flops 230622528 | bytes 7670016 | tf_op jit(solution)/shard_map/hij,sjhd->sihd/dot_general | solution.py:149
  496.9 192.6 %all-reduce.11.cloned.1.call-done = (bf16[4,768,12,64]{3,0,2,1:T(4,128)(2,1)}, bf16[4,768,12,64]{3,0,2,1:T(4,128)(2,1)}) async-done(((bf16[4,768,12,64]{3,0,2,1:T(4,128)(2,1)}, bf16[4,768,12,64]{3,0,2,1:T(4,128)(2,1)}), (bf16[4,768,12,64]{3,0,2,1:T(4,128)(2,1)}, bf16[4,768,12,64]{3,0,2,1:T(4,128)(2,1)})) %all-reduce.11.cloned.1.call-update) | async-done | bytes 9437200
  (162 shorter events, 81.8 us)
Async XLA Ops:
  7.2 235.0 %copy-start = (bf16[768,768]{1,0:T(8,128)(2,1)S(1)}, bf16[768,768]{1,0:T(8,128)(2,1)}, u32[]{:S(2)}) copy-start(bf16[768,768]{1,0:T(8,128)(2,1)} %param.22) | copy-start | bytes 3538948
  7.2 5.2 copy-start.8
  7.2 69.6 %all-gather.5.cloned.1.call-start = ((), (), s32[]{:S(2)}) async-start(), calls=%async_computation.9 | async-start | bytes 10027008 | tf_op jit(solution)/shard_map/all_gather | solution.py:59
  10.4 1.9 copy-start.23
  15.9 151.9 %all-reduce.7.cloned.1.call-start = ((), (), s32[]{:S(2)}) async-start(), calls=%async_computation.10 | async-start | bytes 1769472 | tf_op jit(solution)/shard_map/psum | solution.py:64
  19.0 65.3 %copy-start.13 = (bf16[4,48,12,64]{3,2,1,0:T(8,128)(2,1)}, bf16[4,48,12,64]{3,2,1,0:T(8,128)(2,1)S(1)}, u32[]{:S(2)}) copy-start(bf16[4,48,12,64]{3,2,1,0:T(8,128)(2,1)S(1)} %reshape.173) | copy-start | bytes 884740
  19.0 65.3 %copy-start.10 = (bf16[768,768]{1,0:T(8,128)(2,1)S(1)}, bf16[768,768]{1,0:T(8,128)(2,1)}, u32[]{:S(2)}) copy-start(bf16[768,768]{1,0:T(8,128)(2,1)} %param.17) | copy-start | bytes 3538948
  84.3 145.8 %all-gather.3.cloned.1.call-start = ((), (), s32[]{:S(2)}) async-start(), calls=%async_computation.8 | async-start | bytes 10027008 | tf_op jit(solution)/shard_map/all_gather | solution.py:60
  88.2 155.3 %all-to-all-start.4 = ((bf16[4,48,768]{2,0,1:T(4,128)(2,1)}), bf16[4,48,768]{2,0,1:T(4,128)(2,1)S(1)}, u32[]{:S(2)}, u32[]{:S(2)}) async-start(bf16[4,48,768]{2,0,1:T(4,128)(2,1)} %copy.75), calls=%async_computation.4 | async-start | bytes 589824 | tf_op jit(solution)/shard_map/all_to_all | solution.py:108
  171.0 65.2 %copy-start.30 = (f32[12,48]{1,0:T(8,128)}, f32[12,48]{1,0:T(8,128)S(1)}, u32[]{:S(2)}) copy-start(f32[12,48]{1,0:T(8,128)S(1)} %get-tuple-element.8) | copy-start | bytes 6916
  236.2 3.7 copy-start.2
  236.2 3.7 copy-start.3
  239.9 2.2 copy-start.21
  243.5 14.4 %all-to-all-start = ((bf16[4,48,768]{2,0,1:T(4,128)(2,1)}), bf16[4,48,768]{2,0,1:T(4,128)(2,1)}, u32[]{:S(2)}, u32[]{:S(2)}) async-start(bf16[4,48,768]{2,0,1:T(4,128)(2,1)} %copy.62), calls=%async_computation | async-start | bytes 589824 | tf_op jit(solution)/shard_map/all_to_all | solution.py:80
  257.9 12.2 %all-to-all-start.2 = ((bf16[4,48,768]{2,0,1:T(4,128)(2,1)}), bf16[4,48,768]{2,0,1:T(4,128)(2,1)}, u32[]{:S(2)}, u32[]{:S(2)}) async-start(bf16[4,48,768]{2,0,1:T(4,128)(2,1)} %copy.66), calls=%async_computation.2 | async-start | bytes 589824 | tf_op jit(solution)/shard_map/all_to_all | solution.py:79
  270.0 12.3 %all-to-all-start.1 = ((bf16[4,48,768]{2,0,1:T(4,128)(2,1)}), bf16[4,48,768]{2,0,1:T(4,128)(2,1)}, u32[]{:S(2)}, u32[]{:S(2)}) async-start(bf16[4,48,768]{2,0,1:T(4,128)(2,1)} %copy.64), calls=%async_computation.1 | async-start | bytes 589824 | tf_op jit(solution)/shard_map/all_to_all | solution.py:78
  287.8 33.2 %copy-start.32 = (f32[6,12,32]{2,1,0:T(8,128)}, f32[6,12,32]{2,1,0:T(8,128)S(1)}, u32[]{:S(2)}) copy-start(f32[6,12,32]{2,1,0:T(8,128)S(1)} %get-tuple-element.12) | copy-start | bytes 27652
  299.3 15.0 %all-to-all-start.5 = ((bf16[32,6,768]{2,1,0:T(8,128)(2,1)}), bf16[32,6,768]{2,1,0:T(8,128)(2,1)}, u32[]{:S(2)}, u32[]{:S(2)}) async-start(bf16[32,6,768]{2,1,0:T(8,128)(2,1)} %reshape.204), calls=%async_computation.5 | async-start | bytes 786432 | tf_op jit(solution)/shard_map/all_to_all | solution.py:126
  314.3 14.9 %all-to-all-start.6 = ((bf16[32,6,768]{2,1,0:T(8,128)(2,1)}), bf16[32,6,768]{2,1,0:T(8,128)(2,1)}, u32[]{:S(2)}, u32[]{:S(2)}) async-start(bf16[32,6,768]{2,1,0:T(8,128)(2,1)} %reshape.205), calls=%async_computation.6 | async-start | bytes 786432 | tf_op jit(solution)/shard_map/all_to_all | solution.py:129
  329.3 14.9 %all-to-all-start.7 = ((bf16[32,6,768]{2,1,0:T(8,128)(2,1)}), bf16[32,6,768]{2,1,0:T(8,128)(2,1)}, u32[]{:S(2)}, u32[]{:S(2)}) async-start(bf16[32,6,768]{2,1,0:T(8,128)(2,1)} %reshape.206), calls=%async_computation.7 | async-start | bytes 786432 | tf_op jit(solution)/shard_map/all_to_all | solution.py:132
  335.9 110.2 %all-reduce.9.cloned.1.call-start = ((), (), s32[]{:S(2)}) async-start(), calls=%async_computation.11 | async-start | bytes 1769472 | tf_op jit(solution)/shard_map/psum | solution.py:147
  342.5 5.3 copy-start.19
  347.7 2.0 copy-start.20
  352.6 7.7 %copy-start.31 = (f32[12,48]{1,0:T(8,128)S(1)}, f32[12,48]{1,0:T(8,128)}, u32[]{:S(2)}) copy-start(f32[12,48]{1,0:T(8,128)} %copy-done.30) | copy-start | bytes 6916
  360.2 329.4 %all-reduce.11.cloned.1.call-start = ((), (), s32[]{:S(2)}) async-start(), calls=%async_computation.12 | async-start | bytes 37748736
  365.4 80.7 %copy-start.14 = (bf16[4,48,12,64]{3,2,1,0:T(8,128)(2,1)S(1)}, bf16[4,48,12,64]{3,2,1,0:T(8,128)(2,1)}, u32[]{:S(2)}) copy-start(bf16[4,48,12,64]{3,2,1,0:T(8,128)(2,1)} %copy-done.13) | copy-start | bytes 884740
  471.6 5.1 copy-start.29
  472.9 11.8 %copy-start.5 = (bf16[768,768]{1,0:T(8,128)(2,1)S(1)}, bf16[768,768]{1,0:T(8,128)(2,1)}, u32[]{:S(2)}) copy-start(bf16[768,768]{1,0:T(8,128)(2,1)} %param.23) | copy-start | bytes 3538948
  472.9 11.7 %all-to-all-start.3 = ((bf16[32,6,768]{2,1,0:T(8,128)(2,1)}), bf16[32,6,768]{2,1,0:T(8,128)(2,1)S(1)}, u32[]{:S(2)}, u32[]{:S(2)}) async-start(bf16[32,6,768]{2,1,0:T(8,128)(2,1)} %reshape.203), calls=%async_computation.3 | async-start | bytes 786432 | tf_op jit(solution)/shard_map/all_to_all | solution.py:96
  693.9 1.6 copy-start.11
  693.9 1.7 copy-start.15
  693.9 1.7 copy-start.22
  (15 other events, 16.0 us)
Sparse Core Ops, SparseCore 0:
  16.1 60.6 all-gather.4
  84.4 83.3 all-reduce.6
  169.6 60.4 all-gather.2
  360.3 85.7 all-reduce.8
  468.7 220.7 all-reduce.10
where the time goes:
time: 708 us; the launch traced here: 704 us
  waiting for transfers between devices  467 us (66%)
  local copies, waits for them, and re-layouts  89 us (13%)
  matrix products  78.5 us (11%)
  starting transfers between devices  45.5 us (6%)
  between operations  15 us (2%)
  other arithmetic  9.34 us (1%)
    unnamed x6, waiting for transfers between devices  193 us
    psum x1, waiting for transfers between devices, local(): lax.psum(partial_logits.astype(jnp.bfloat16), 'seq').astype(jnp.float32)  73.1 us
    psum x1, waiting for transfers between devices, local(): lax.psum(partial_grads.astype(jnp.bfloat16), 'seq').astype(jnp.float32)  65.3 us
    all_gather x1, waiting for transfers between devices, local(): lax.all_gather(row_value, 'res', axis=1, tiled=True)  59.1 us
    all_gather x1, waiting for transfers between devices, local(): lax.all_gather(row_key, 'res', axis=1, tiled=True)  57.8 us
    convert_element_type x1, local copies, waits for them, and re-layouts, local(): value_terms.astype(jnp.bfloat16)  15.4 us
    convert_element_type x1, local copies, waits for them, and re-layouts, local(): key_terms.astype(jnp.bfloat16)  15.4 us
  transfers between devices with their start and end apart: 13, of which 9 were waited for; matrix products, arithmetic and copies ran while one was open for 13% of the time, Pallas kernels for 0%

commit v1 on v0

v1 whole, which is shorter than its diff:
```python
import math

import jax
import jax.numpy as jnp
from jax import lax
from jax.experimental import pallas as pl
from jax.experimental.pallas import tpu as pltpu
from jax.sharding import Mesh
from jax.sharding import PartitionSpec as P

F32 = jnp.float32
BF16 = jnp.bfloat16
D = 768
HEADS = 12
HEAD_DIM = 64
SEQ = ("xh", "z")
GRP = ("xl", "c")
WIDE = ("xh", "z", "xl", "c")
ALLRES = ("y", "xl", "c")
NS, NG, NY = 8, 4, 4
GH = HEADS // NG
S = 4
R = 48
I = R * NG
CR = 6
CP = 8
TOK = NS * S * CP
ROWS = GH * I // NS
WIDTH = GH * S * HEAD_DIM
ROW_SCALE = 1.0 / math.sqrt(HEAD_DIM * 32)
COL_SCALE = 1.0 / math.sqrt(HEAD_DIM)


def dot(a, b):
    return lax.dot_general(a, b, (((1,), (0,)), ((), ())), preferred_element_type=F32)


def dot_nt(a, b):
    return lax.dot_general(a, b, (((1,), (1,)), ((), ())), preferred_element_type=F32)


def dot_tn(a, b):
    return lax.dot_general(a, b, (((0,), (0,)), ((), ())), preferred_element_type=F32)


def call(kernel, outs, *args, mem=32, scratch=()):
    shapes = [jax.ShapeDtypeStruct(s, t) for s, t in outs]
    res = pl.pallas_call(
        kernel,
        out_shape=shapes,
        in_specs=[pl.BlockSpec(memory_space=pltpu.VMEM)] * len(args),
        out_specs=[pl.BlockSpec(memory_space=pltpu.VMEM)] * len(outs),
        scratch_shapes=list(scratch),
        compiler_params=pltpu.CompilerParams(vmem_limit_bytes=mem * 2**20),
    )(*args)
    return res[0] if len(outs) == 1 else res


def halves(a, b, half_a, half_b):
    low = lax.broadcasted_iota(jnp.int32, a.shape, 1) < 64
    a = a if half_a == 0 else pltpu.roll(a, 64, 1)
    b = b if half_b == 1 else pltpu.roll(b, 64, 1)
    return jnp.where(low, a, b)


def blk(v, n):
    return v[:, n * 128 : (n + 1) * 128]


def to_column():
    row = lax.broadcasted_iota(jnp.int32, (TOK, S * R), 0)
    col = lax.broadcasted_iota(jnp.int32, (TOK, S * R), 1)
    r = row % CP
    want = ((row // CP) % S) * R + (row // (CP * S)) * CR + r
    return jnp.where((r < CR) & (col == want), 1.0, 0.0).astype(BF16)


def to_wide():
    row = lax.broadcasted_iota(jnp.int32, (TOK, I), 0)
    col = lax.broadcasted_iota(jnp.int32, (TOK, I), 1)
    r = row % CP
    want = ((row // CP) % NG) * R + (row // (CP * NG)) * CR + r
    return jnp.where((r < CR) & (col == want), 1.0, 0.0).astype(BF16)


def moments(v):
    mean = jnp.mean(v, axis=-1, keepdims=True)
    centred = v - mean
    r = lax.rsqrt(jnp.mean(centred * centred, axis=-1, keepdims=True) + 1e-05)
    return centred * r, r


def norm_grad(grad, gain, hat, r):
    g = grad * gain
    return r * (
        g - jnp.mean(g, axis=-1, keepdims=True) - hat * jnp.mean(g * hat, axis=-1, keepdims=True)
    )


def k_send(x, cot, out):
    perm = to_column()
    a = dot(perm, x[...].astype(F32).reshape(S * R, D).astype(BF16)).astype(BF16)
    b = dot(perm, cot[...].astype(F32).reshape(S * R, D).astype(BF16)).astype(BF16)
    out[:, 0:D] = a
    out[:, D : 2 * D] = b


def k_project(x, gain, wq, wk, wv, keys, qv):
    hat, _ = moments(x[...].astype(F32).reshape(S * R, D))
    normed = (hat * gain[...]).astype(BF16)
    for which, w in enumerate((wk, wq, wv)):
        y = dot(normed, w[...])
        for g in range(NG):
            for h in range(GH):
                n = g * GH + h
                src = blk(y, n // 2)
                for sp in range(2):
                    a = src[2 * sp * R : (2 * sp + 1) * R]
                    b = src[(2 * sp + 1) * R : (2 * sp + 2) * R]
                    piece = halves(a, b, n % 2, n % 2).astype(BF16)
                    at = h * 256 + sp * 128
                    if which == 0:
                        for yy in range(NY):
                            keys[yy * NG + g, :, at : at + 128] = piece
                    else:
                        at = at + (which - 1) * WIDTH
                        qv[g, :, at : at + 128] = piece


def k_logits(qv, keys, out):
    tops = []
    for h in range(GH):
        c = slice(h * 256, (h + 1) * 256)
        tops.append(dot_nt(qv[:, c], keys[:, c]))
    full = jnp.concatenate(tops, axis=0)
    for a in range(NS):
        out[a] = full[a * ROWS : (a + 1) * ROWS].astype(BF16)


def summed(parts):
    total = parts[0].astype(F32)
    for a in range(1, parts.shape[0]):
        total = total + parts[a].astype(F32)
    return total


def k_softmax(parts, probs, weights):
    logits = summed(parts) * ROW_SCALE
    e = jnp.exp(logits - jnp.max(logits, axis=-1, keepdims=True))
    p = e / jnp.sum(e, axis=-1, keepdims=True)
    probs[...] = p
    w = p.astype(BF16)
    for a in range(NS):
        weights[a] = w


def k_attend(weights, values, out):
    perm = to_wide()
    for h in range(GH):
        c = slice(h * 256, (h + 1) * 256)
        att = dot(weights[h * I : (h + 1) * I], values[:, c]).astype(BF16)
        out[:, c] = dot(perm, att).astype(BF16)


def k_column(
    att_in, xc, gain, out_row, wq, wk, wv, out_col, back, grad_out, att_s, gq_s, gk_s, gv_s
):
    raw = att_in[...].astype(F32).reshape(NS, NG, CP, WIDTH)
    groups = [raw[:, g].reshape(NS * CP, WIDTH) for g in range(NG)]
    per_seq = []
    for s in range(S):
        cols = []
        for fb in range(6):
            pair = []
            for n in (2 * fb, 2 * fb + 1):
                pair.append(blk(groups[n // GH], (n % GH) * 2 + s // 2))
            cols.append(halves(pair[0], pair[1], s % 2, s % 2))
        per_seq.append(jnp.concatenate(cols, axis=1).reshape(NS, 1, CP, D))
    att_row = jnp.concatenate(per_seq, axis=1).reshape(TOK, D).astype(BF16)
    middle = (xc[:, 0:D].astype(F32) + dot(att_row, out_row[...])).astype(BF16)
    mid = middle.astype(F32)
    cot = xc[:, D : 2 * D]
    hat, r = moments(mid)
    normed = (hat * gain[...]).astype(BF16)
    q = dot(normed, wq[...]).astype(BF16)
    k = dot(normed, wk[...]).astype(BF16)
    v = dot(normed, wv[...]).astype(BF16)
    ga = dot_nt(cot, out_col[...]).astype(BF16)
    row = lax.broadcasted_iota(jnp.int32, (TOK, TOK), 0)
    col = lax.broadcasted_iota(jnp.int32, (TOK, TOK), 1)
    same = (row % CP) == (col % CP)
    lane = lax.broadcasted_iota(jnp.int32, (1, 128), 1)
    for fb in range(6):
        qb, kb, vb, gb = (blk(t, fb) for t in (q, k, v, ga))
        att = gq = gk = gv = None
        for half in range(2):
            mask = jnp.where((lane < 64) == (half == 0), 1.0, 0.0).astype(BF16)
            km, vm, qm, gm = kb * mask, vb * mask, qb * mask, gb * mask
            logits = jnp.where(same, dot_nt(qb, km) * COL_SCALE, -1e30)
            e = jnp.exp(logits - jnp.max(logits, axis=-1, keepdims=True))
            p = e / jnp.sum(e, axis=-1, keepdims=True)
            w = p.astype(BF16)
            grads = dot_nt(gb, vm)
            dl = p * (grads - jnp.sum(p * grads, axis=-1, keepdims=True)) * COL_SCALE
            dl = dl.astype(BF16)
            parts = (dot(w, vm), dot(dl, km), dot_tn(dl, qm), dot_tn(w, gm))
            if half == 0:
                att, gq, gk, gv = parts
            else:
                att, gq, gk, gv = (t + u for t, u in zip((att, gq, gk, gv), parts))
        at = slice(fb * 128, (fb + 1) * 128)
        att_s[:, at] = att.astype(BF16)
        gq_s[:, at] = gq.astype(BF16)
        gk_s[:, at] = gk.astype(BF16)
        gv_s[:, at] = gv.astype(BF16)
    back[:, 0:D] = (mid + dot(att_s[...], out_col[...])).astype(BF16)
    gn = (
        dot_nt(gq_s[...], wq[...]) + dot_nt(gk_s[...], wk[...]) + dot_nt(gv_s[...], wv[...])
    )
    gmid = (cot.astype(F32) + norm_grad(gn, gain[...], hat, r)).astype(BF16)
    back[:, D : 2 * D] = gmid
    gra = dot_nt(gmid, out_row[...]).reshape(NS, S, CP, D)
    seqs = [gra[:, s].reshape(NS * CP, D) for s in range(S)]
    per_group = []
    for g in range(NG):
        cols = []
        for h in range(GH):
            n = g * GH + h
            for sp in range(2):
                cols.append(
                    halves(blk(seqs[2 * sp], n // 2), blk(seqs[2 * sp + 1], n // 2), n % 2, n % 2)
                )
        per_group.append(jnp.concatenate(cols, axis=1).reshape(NS, 1, CP, WIDTH))
    grad_out[...] = jnp.concatenate(per_group, axis=1).reshape(TOK, WIDTH).astype(BF16)


def k_grad_probs(grads, values, gra, out):
    perm = to_wide()
    tops = []
    for h in range(GH):
        c = slice(h * 256, (h + 1) * 256)
        g = dot_tn(perm, grads[:, c]).astype(BF16)
        gra[:, c] = g
        tops.append(dot_nt(g, values[:, c]))
    full = jnp.concatenate(tops, axis=0)
    for a in range(NS):
        out[a] = full[a * ROWS : (a + 1) * ROWS].astype(BF16)


def k_grad_values(weights, gra, out):
    for h in range(GH):
        c = slice(h * 256, (h + 1) * 256)
        out[:, c] = dot_tn(weights[h * I : (h + 1) * I], gra[:, c]).astype(BF16)


def k_softmax_grad(parts, probs, out):
    grads = summed(parts)
    p = probs[...]
    dl = p * (grads - jnp.sum(p * grads, axis=-1, keepdims=True)) * ROW_SCALE
    dl = dl.astype(BF16)
    for a in range(NS):
        out[a] = dl


def k_grad_qk(dl, keys, qv, gq, gk):
    for h in range(GH):
        c = slice(h * 256, (h + 1) * 256)
        d = dl[h * I : (h + 1) * I]
        gk[:, c] = dot_tn(d, qv[:, c]).astype(BF16)
        gq[:, c] = dot(d, keys[:, c]).astype(BF16)


def k_finish(gq, gk, gv, x, back, gain, wq, wk, wv, block_out, input_grad):
    total = None
    for kind, w in ((0, wq), (1, wk), (2, wv)):
        groups = []
        for g in range(NG):
            if kind == 0:
                t = gq[g].astype(F32)
            elif kind == 2:
                t = gv[g].astype(F32)
            else:
                t = gk[g].astype(F32)
                for yy in range(1, NY):
                    t = t + gk[yy * NG + g].astype(F32)
            groups.append(t)
        rows = []
        for s in range(S):
            cols = []
            for fb in range(6):
                pair = []
                for n in (2 * fb, 2 * fb + 1):
                    pair.append(blk(groups[n // GH], (n % GH) * 2 + s // 2))
                cols.append(halves(pair[0], pair[1], s % 2, s % 2))
            rows.append(jnp.concatenate(cols, axis=1))
        t = dot_nt(jnp.concatenate(rows, axis=0).astype(BF16), w[...])
        total = t if total is None else total + t
    perm = to_column()
    bo = dot_tn(perm, back[:, 0:D])
    gmid = dot_tn(perm, back[:, D : 2 * D])
    hat, r = moments(x[...].astype(F32).reshape(S * R, D))
    block_out[...] = bo.reshape(S, R, D).astype(BF16)
    grad = gmid + norm_grad(total, gain[...], hat, r)
    input_grad[...] = grad.reshape(S, R, D).astype(BF16)


def swap(x, axes):
    return lax.all_to_all(x, axes, split_axis=0, concat_axis=0, tiled=True)


def local(
    x,
    cot,
    gain_row,
    query_row,
    key_row,
    value_row,
    out_row,
    gain_col,
    query_col,
    key_col,
    value_col,
    out_col,
):
    gain_row = gain_row.reshape(1, D)
    gain_col = gain_col.reshape(1, D)
    keys, qv = call(
        k_project,
        [((NY * NG, R, WIDTH), BF16), ((NG, R, 2 * WIDTH), BF16)],
        x, gain_row, query_row, key_row, value_row,
    )
    keys = swap(keys, ALLRES).reshape(NY * I, WIDTH)
    qv = swap(qv, GRP).reshape(I, 2 * WIDTH)
    values = lax.all_gather(qv[:, WIDTH:], "y", axis=0, tiled=True)
    sent = call(k_send, [((TOK, 2 * D), BF16)], x, cot)
    xc = swap(sent, SEQ)
    parts = swap(call(k_logits, [((NS, ROWS, NY * I), BF16)], qv, keys), SEQ)
    probs, weights = call(
        k_softmax, [((ROWS, NY * I), F32), ((NS, ROWS, NY * I), BF16)], parts
    )
    weights = swap(weights, SEQ).reshape(GH * I, NY * I)
    att = swap(call(k_attend, [((TOK, WIDTH), BF16)], weights, values), WIDE)
    back, grads = call(
        k_column,
        [((TOK, 2 * D), BF16), ((TOK, WIDTH), BF16)],
        att, xc, gain_col, out_row, query_col, key_col, value_col, out_col,
        mem=48,
        scratch=[pltpu.VMEM((TOK, D), BF16)] * 4,
    )
    grads = swap(grads, WIDE)
    gra, gparts = call(
        k_grad_probs, [((I, WIDTH), BF16), ((NS, ROWS, NY * I), BF16)], grads, values
    )
    gparts = swap(gparts, SEQ)
    gv = call(k_grad_values, [((NY * I, WIDTH), BF16)], weights, gra)
    gv = lax.psum_scatter(gv, "y", scatter_dimension=0, tiled=True)
    dl = call(k_softmax_grad, [((NS, ROWS, NY * I), BF16)], gparts, probs)
    dl = swap(dl, SEQ).reshape(GH * I, NY * I)
    back = swap(back, SEQ)
    gq, gk = call(
        k_grad_qk, [((I, WIDTH), BF16), ((NY * I, WIDTH), BF16)], dl, keys, qv
    )
    gk = swap(gk, ALLRES).reshape(NY * NG, R, WIDTH)
    gq = swap(gq, GRP).reshape(NG, R, WIDTH)
    gv = swap(gv, GRP).reshape(NG, R, WIDTH)
    return call(
        k_finish,
        [((S, R, D), BF16), ((S, R, D), BF16)],
        gq, gk, gv, x, back, gain_row, query_row, key_row, value_row,
    )


def solution(mesh):
    fine = Mesh(mesh.devices.reshape(2, 4, 2, 4, 2), ("xh", "z", "xl", "y", "c"))
    spec = P(("xh", "z"), ("xl", "y", "c"), None)
    return jax.shard_map(
        local,
        mesh=fine,
        in_specs=(spec, spec) + (P(),) * 10,
        out_specs=(spec, spec),
        check_vma=False,
    )
```

time: 708 us -> 263 us (0.37)
  waiting for transfers between devices: 467 us -> 58.7 us
  blocking collectives: 0 us -> 115 us
  matrix products: 78.5 us -> 0 us
  local copies, waits for them, and re-layouts: 89 us -> 20 us
  Pallas kernels: 0 us -> 20.9 us
  starting transfers between devices: 45.5 us -> 33.1 us
  other arithmetic: 9.34 us -> 0 us
    unnamed x6 -> x2, waiting for transfers between devices: 193 us -> 0.03 us
    psum x2 -> x0, waiting for transfers between devices: 138 us -> none  [the longest x1 73.1 us: local(): lax.psum(partial_logits.astype(jnp.bfloat16), 'seq').astype(jnp.float32)]
    all_gather x2 -> x1, waiting for transfers between devices: 117 us -> 0.01 us  [local(): values = lax.all_gather(qv[:, WIDTH:], 'y', axis=0, tiled=True)]
    all_to_all x0 -> x7, blocking collectives: none -> 115 us  [swap(): return lax.all_to_all(x, axes, split_axis=0, concat_axis=0, tiled=True)]
    dot_general x27 -> x0, matrix products: 75.5 us -> none  [the longest x8 10.2 us: back_project(): return jnp.dot(flat, weight.T, preferred_element_type=jnp.float32)]
    all_to_all x8 -> x6, waiting for transfers between devices: 18.8 us -> 58.6 us  [swap(): return lax.all_to_all(x, axes, split_axis=0, concat_axis=0, tiled=True)]
    reshape x30 -> x2, local copies, waits for them, and re-layouts: 39.2 us -> 0.69 us  [the longest x1 0.69 us: local(): gain_row = gain_row.reshape(1, D)]
    convert_element_type x4 -> x0, local copies, waits for them, and re-layouts: 32.6 us -> none  [the longest x1 15.4 us: local(): value_terms.astype(jnp.bfloat16)]
  transfers between devices with their start and end apart: 13 -> 8, of which waited for: 9 -> 6; matrix products, arithmetic and copies ran while one was open for 13% -> 0% of each run, Pallas kernels for 0% -> 2%
where the time goes in v1:
time: 263 us; the launch traced here: 262 us
  blocking collectives  115 us (44%)
  waiting for transfers between devices  58.7 us (22%)
  starting transfers between devices  33.1 us (13%)
  Pallas kernels  20.9 us (8%)
  local copies, waits for them, and re-layouts  20 us (8%)
  between operations  14.3 us (5%)
    all_to_all x7, blocking collectives, swap(): return lax.all_to_all(x, axes, split_axis=0, concat_axis=0, tiled=True)  115 us
    all_to_all x6, waiting for transfers between devices, swap(): return lax.all_to_all(x, axes, split_axis=0, concat_axis=0, tiled=True)  58.6 us
    all_to_all x6, starting transfers between devices, swap(): return lax.all_to_all(x, axes, split_axis=0, concat_axis=0, tiled=True)  33 us
    pallas_call x11, Pallas kernels, call(): pl.pallas_call(kernel, out_shape=shapes, in_specs=[pl.BlockSpec(memory_sp...  20.9 us
    unnamed x54, local copies, waits for them, and re-layouts  18.6 us
  transfers between devices with their start and end apart: 8, of which 6 were waited for; matrix products, arithmetic and copies ran while one was open for 0% of the time, Pallas kernels for 2%

profile of v1, /device:TPU:1, one launch (start us, length us, event | category | flops | bytes accessed | tf_op | source)
XLA Modules:
  0.0 261.9 jit_solution(10069240839251384034)
XLA Ops:
  7.9 1.3 copy-done
  9.1 1.3 copy-done.2
  10.4 1.3 copy-done.4
  12.6 1.1 shard_map.131
  13.8 12.9 %all_to_all.101 = bf16[4,48,1536]{2,1,0:T(8,128)(2,1)S(1)} all-to-all(bf16[4,48,1536]{2,1,0:T(8,128)(2,1)S(1)} %get-tuple-element.12), channel_id=1, replica_groups=mesh['xh'=2,'z'=4,'xl'=2,'y'=4,'c'=2] {'xl','c'}, dimensions={0} | all-to-all | bytes 1179648 | tf_op jit(solution)/shard_map/all_to_all | solution.py:308
  26.6 22.4 %all_to_all.102 = bf16[16,48,768]{2,1,0:T(8,128)(2,1)S(1)} all-to-all(bf16[16,48,768]{2,1,0:T(8,128)(2,1)S(1)} %get-tuple-element.13), channel_id=1, replica_groups=mesh['xh'=2,'z'=4,'xl'=2,'y'=4,'c'=2] {'y','xl','c'}, dimensions={0} | all-to-all | bytes 2359296 | tf_op jit(solution)/shard_map/all_to_all | solution.py:308
  49.0 1.5 shard_map.132
  50.5 7.3 %all-to-all-start.2 = ((bf16[8,72,768]{2,1,0:T(8,128)(2,1)}), bf16[8,72,768]{2,1,0:T(8,128)(2,1)S(1)}, u32[]{:S(2)}, u32[]{:S(2)}) async-start(bf16[8,72,768]{2,1,0:T(8,128)(2,1)} %shard_map.132), calls=%async_computation.2 | async-start | bytes 1769472 | tf_op jit(solution)/shard_map/all_to_all | solution.py:308
  58.6 11.6 %all-to-all-done.2.parts = bf16[8,72,768]{2,1,0:T(8,128)(2,1)S(1)} async-done(((bf16[8,72,768]{2,1,0:T(8,128)(2,1)}), bf16[8,72,768]{2,1,0:T(8,128)(2,1)S(1)}, u32[]{:S(2)}, u32[]{:S(2)}) %all-to-all-start.2) | async-done | bytes 884768 | tf_op jit(solution)/shard_map/all_to_all | solution.py:308
  72.2 5.9 %all-to-all-start.3 = ((bf16[8,72,768]{2,1,0:T(8,128)(2,1)}), bf16[8,72,768]{2,1,0:T(8,128)(2,1)S(1)}, u32[]{:S(2)}, u32[]{:S(2)}) async-start(bf16[8,72,768]{2,1,0:T(8,128)(2,1)} %copy-done.18), calls=%async_computation.3 | async-start | bytes 1769472 | tf_op jit(solution)/shard_map/all_to_all | solution.py:308
  78.1 1.3 shard_map.135
  79.4 11.4 %all-to-all-done.3 = bf16[8,72,768]{2,1,0:T(8,128)(2,1)S(1)} async-done(((bf16[8,72,768]{2,1,0:T(8,128)(2,1)}), bf16[8,72,768]{2,1,0:T(8,128)(2,1)S(1)}, u32[]{:S(2)}, u32[]{:S(2)}) %all-to-all-start.3) | async-done | bytes 884768 | tf_op jit(solution)/shard_map/all_to_all | solution.py:308
  90.7 5.7 %all-to-all-start.5 = ((bf16[8,32,1536]{2,1,0:T(8,128)(2,1)}), bf16[8,32,1536]{2,1,0:T(8,128)(2,1)S(1)}, u32[]{:S(2)}, u32[]{:S(2)}) async-start(bf16[8,32,1536]{2,1,0:T(8,128)(2,1)} %bitcast.5), calls=%async_computation.5 | async-start | bytes 1572864 | tf_op jit(solution)/shard_map/all_to_all | solution.py:308
  96.5 1.3 copy-done.6
  97.8 1.0 shard_map.134
  99.6 8.5 %all-to-all-done.5 = bf16[8,32,1536]{2,1,0:T(8,128)(2,1)S(1)} async-done(((bf16[8,32,1536]{2,1,0:T(8,128)(2,1)}), bf16[8,32,1536]{2,1,0:T(8,128)(2,1)S(1)}, u32[]{:S(2)}, u32[]{:S(2)}) %all-to-all-start.5) | async-done | bytes 786464 | tf_op jit(solution)/shard_map/all_to_all | solution.py:308
  108.1 6.9 %all-to-all-start.4 = ((bf16[32,8,768]{2,1,0:T(8,128)(2,1)}), bf16[32,8,768]{2,1,0:T(8,128)(2,1)}, u32[]{:S(2)}, u32[]{:S(2)}) async-start(bf16[32,8,768]{2,1,0:T(8,128)(2,1)} %bitcast.25), calls=%async_computation.4 | async-start | bytes 786432 | tf_op jit(solution)/shard_map/all_to_all | solution.py:308
  115.0 10.0 %all-to-all-done.4 = bf16[32,8,768]{2,1,0:T(8,128)(2,1)} async-done(((bf16[32,8,768]{2,1,0:T(8,128)(2,1)}), bf16[32,8,768]{2,1,0:T(8,128)(2,1)}, u32[]{:S(2)}, u32[]{:S(2)}) %all-to-all-start.4) | async-done | bytes 393248 | tf_op jit(solution)/shard_map/all_to_all | solution.py:308
  125.0 1.3 copy-done.14
  126.3 1.3 copy-done.15
  127.6 1.3 copy-done.16
  128.8 11.1 %shard_map.136 = (bf16[256,1536]{1,0:T(8,128)(2,1)S(1)}, bf16[256,768]{1,0:T(8,128)(2,1)S(1)}) custom-call(bf16[256,768]{1,0:T(8,128)(2,1)} %bitcast.4.att_in, bf16[256,1536]{1,0:T(8,128)(2,1)S(1)} %bitcast.24, f32[1,768]{1,0:T(1,128)S(1)} %reshape.46.gain, bf16[768,768]{1,0:T(8,128)(2,1)S(1)} %copy-done.14, bf16[768,768]{1,0:T(8,128)(2,1)S(1)} %copy-done.15, ...), custom_call_target="tpu_custom_call" | custom-call | tf_op jit(solution)/shard_map/pallas_call | solution.py:48
  140.0 14.1 %all_to_all.103 = bf16[32,8,768]{2,1,0:T(8,128)(2,1)S(1)} all-to-all(bf16[32,8,768]{2,1,0:T(8,128)(2,1)S(1)} %bitcast.29), channel_id=1, replica_groups=mesh['xh'=2,'z'=4,'xl'=2,'y'=4,'c'=2] {'xh','z','xl','c'}, dimensions={0} | all-to-all | bytes 786432 | tf_op jit(solution)/shard_map/all_to_all | solution.py:308
  156.6 3.5 %all-to-all-start.7 = ((bf16[8,72,768]{2,1,0:T(8,128)(2,1)}), bf16[8,72,768]{2,1,0:T(8,128)(2,1)S(1)}, u32[]{:S(2)}, u32[]{:S(2)}) async-start(bf16[8,72,768]{2,1,0:T(8,128)(2,1)} %copy-done.17), calls=%async_computation.7 | async-start | bytes 1769472 | tf_op jit(solution)/shard_map/all_to_all | solution.py:308
  162.8 9.6 %all-to-all-done.7.parts = bf16[8,72,768]{2,1,0:T(8,128)(2,1)S(1)} async-done(((bf16[8,72,768]{2,1,0:T(8,128)(2,1)}), bf16[8,72,768]{2,1,0:T(8,128)(2,1)S(1)}, u32[]{:S(2)}, u32[]{:S(2)}) %all-to-all-start.7) | async-done | bytes 884768 | tf_op jit(solution)/shard_map/all_to_all | solution.py:308
  172.6 20.3 %all_to_all.104 = bf16[8,72,768]{2,1,0:T(8,128)(2,1)S(1)} all-to-all(bf16[8,72,768]{2,1,0:T(8,128)(2,1)S(1)} %shard_map.138), channel_id=1, replica_groups=mesh['xh'=2,'z'=4,'xl'=2,'y'=4,'c'=2] {'xh','z'}, dimensions={0} | all-to-all | bytes 1769472 | tf_op jit(solution)/shard_map/all_to_all | solution.py:308
  192.9 3.5 %all-to-all-start.12 = ((bf16[8,32,1536]{2,1,0:T(8,128)(2,1)}), bf16[8,32,1536]{2,1,0:T(8,128)(2,1)S(1)}, u32[]{:S(2)}, u32[]{:S(2)}) async-start(bf16[8,32,1536]{2,1,0:T(8,128)(2,1)} %bitcast.28), calls=%async_computation.13 | async-start | bytes 1572864 | tf_op jit(solution)/shard_map/all_to_all | solution.py:308
  199.0 7.6 %all-to-all-done.12 = bf16[8,32,1536]{2,1,0:T(8,128)(2,1)S(1)} async-done(((bf16[8,32,1536]{2,1,0:T(8,128)(2,1)}), bf16[8,32,1536]{2,1,0:T(8,128)(2,1)S(1)}, u32[]{:S(2)}, u32[]{:S(2)}) %all-to-all-start.12) | async-done | bytes 786464 | tf_op jit(solution)/shard_map/all_to_all | solution.py:308
  206.5 13.8 %all_to_all.105.gq = bf16[4,48,768]{2,1,0:T(8,128)(2,1)S(1)} all-to-all(bf16[4,48,768]{2,1,0:T(8,128)(2,1)} %bitcast.30), channel_id=1, replica_groups=mesh['xh'=2,'z'=4,'xl'=2,'y'=4,'c'=2] {'xl','c'}, dimensions={0} | all-to-all | bytes 589824 | tf_op jit(solution)/shard_map/all_to_all | solution.py:308
  220.4 9.8 %all_to_all.106.gv = bf16[4,48,768]{2,1,0:T(8,128)(2,1)S(1)} all-to-all(bf16[4,48,768]{2,1,0:T(8,128)(2,1)} %bitcast.31), channel_id=1, replica_groups=mesh['xh'=2,'z'=4,'xl'=2,'y'=4,'c'=2] {'xl','c'}, dimensions={0} | all-to-all | bytes 589824 | tf_op jit(solution)/shard_map/all_to_all | solution.py:308
  230.2 21.6 %all_to_all.107.gk = bf16[16,48,768]{2,1,0:T(8,128)(2,1)S(1)} all-to-all(bf16[16,48,768]{2,1,0:T(8,128)(2,1)} %bitcast.27), channel_id=1, replica_groups=mesh['xh'=2,'z'=4,'xl'=2,'y'=4,'c'=2] {'y','xl','c'}, dimensions={0} | all-to-all | bytes 2359296 | tf_op jit(solution)/shard_map/all_to_all | solution.py:308
  252.8 2.3 shard_map.141
  (61 shorter events, 13.9 us)
Async XLA Ops:
  7.9 1.3 copy-start
  9.1 1.3 copy-start.2
  10.4 1.3 copy-start.4
  11.7 1.0 copy-start.9
  50.5 19.8 %all-to-all-start.2 = ((bf16[8,72,768]{2,1,0:T(8,128)(2,1)}), bf16[8,72,768]{2,1,0:T(8,128)(2,1)S(1)}, u32[]{:S(2)}, u32[]{:S(2)}) async-start(bf16[8,72,768]{2,1,0:T(8,128)(2,1)} %shard_map.132), calls=%async_computation.2 | async-start | bytes 1769472 | tf_op jit(solution)/shard_map/all_to_all | solution.py:308
  57.8 38.7 %all-gather.2.cloned.1.call-start = ((), (), s32[]{:S(2)}) async-start(), calls=%async_computation.14 | async-start | bytes 1474560 | tf_op jit(solution)/shard_map/all_gather | solution.py:334
  58.6 19.5 %copy-start.10 = (bf16[4,48,768]{2,1,0:T(8,128)(2,1)S(1)}, bf16[4,48,768]{2,1,0:T(8,128)(2,1)}, u32[]{:S(2)}) copy-start(bf16[4,48,768]{2,1,0:T(8,128)(2,1)} %x.5) | copy-start | bytes 884740
  58.6 19.5 %copy-start.23 = (bf16[4,48,768]{2,1,0:T(8,128)(2,1)S(1)}, bf16[4,48,768]{2,1,0:T(8,128)(2,1)}, u32[]{:S(2)}) copy-start(bf16[4,48,768]{2,1,0:T(8,128)(2,1)} %cot.1) | copy-start | bytes 884740
  70.6 0.9 copy-start.18
  72.2 18.6 %all-to-all-start.3 = ((bf16[8,72,768]{2,1,0:T(8,128)(2,1)}), bf16[8,72,768]{2,1,0:T(8,128)(2,1)S(1)}, u32[]{:S(2)}, u32[]{:S(2)}) async-start(bf16[8,72,768]{2,1,0:T(8,128)(2,1)} %copy-done.18), calls=%async_computation.3 | async-start | bytes 1769472 | tf_op jit(solution)/shard_map/all_to_all | solution.py:308
  90.7 17.3 %all-to-all-start.5 = ((bf16[8,32,1536]{2,1,0:T(8,128)(2,1)}), bf16[8,32,1536]{2,1,0:T(8,128)(2,1)S(1)}, u32[]{:S(2)}, u32[]{:S(2)}) async-start(bf16[8,32,1536]{2,1,0:T(8,128)(2,1)} %bitcast.5), calls=%async_computation.5 | async-start | bytes 1572864 | tf_op jit(solution)/shard_map/all_to_all | solution.py:308
  96.5 1.3 copy-start.6
  97.8 17.2 %copy-start.26 = (f32[768]{0:T(1024)S(1)}, f32[768]{0:T(1024)}, u32[]{:S(2)}) copy-start(f32[768]{0:T(1024)} %param.19) | copy-start | bytes 9220
  98.8 0.8 copy-start.12
  108.1 17.0 %all-to-all-start.4 = ((bf16[32,8,768]{2,1,0:T(8,128)(2,1)}), bf16[32,8,768]{2,1,0:T(8,128)(2,1)}, u32[]{:S(2)}, u32[]{:S(2)}) async-start(bf16[32,8,768]{2,1,0:T(8,128)(2,1)} %bitcast.25), calls=%async_computation.4 | async-start | bytes 786432 | tf_op jit(solution)/shard_map/all_to_all | solution.py:308
  125.0 1.3 copy-start.14
  126.3 1.3 copy-start.15
  127.6 1.3 copy-start.16
  128.8 25.2 %copy-start.7 = (bf16[768,768]{1,0:T(8,128)(2,1)S(1)}, bf16[768,768]{1,0:T(8,128)(2,1)}, u32[]{:S(2)}) copy-start(bf16[768,768]{1,0:T(8,128)(2,1)} %all-gather.2.cloned.1.call-done.values) | copy-start | bytes 3538948
  140.0 14.9 %copy-start.19 = (bf16[256,1536]{1,0:T(8,128)(2,1)}, bf16[256,1536]{1,0:T(8,128)(2,1)S(1)}, u32[]{:S(2)}) copy-start(bf16[256,1536]{1,0:T(8,128)(2,1)S(1)} %get-tuple-element.21) | copy-start | bytes 2359300
  154.9 0.9 copy-start.17
  156.6 15.8 %all-to-all-start.7 = ((bf16[8,72,768]{2,1,0:T(8,128)(2,1)}), bf16[8,72,768]{2,1,0:T(8,128)(2,1)S(1)}, u32[]{:S(2)}, u32[]{:S(2)}) async-start(bf16[8,72,768]{2,1,0:T(8,128)(2,1)} %copy-done.17), calls=%async_computation.7 | async-start | bytes 1769472 | tf_op jit(solution)/shard_map/all_to_all | solution.py:308
  160.1 60.2 %reduce-scatter.2.cloned.1.call-start = ((), (), s32[]{:S(2)}) async-start(), calls=%async_computation.15 | async-start | bytes 1474560 | tf_op jit(solution)/shard_map/reduce_scatter | solution.py:356
  160.2 1.0 copy-start.21
  161.7 1.0 copy-start.8
  162.7 9.7 %copy-start.25 = (f32[72,768]{1,0:T(8,128)S(1)}, f32[72,768]{1,0:T(8,128)}, u32[]{:S(2)}) copy-start(f32[72,768]{1,0:T(8,128)} %copy-done.24) | copy-start | bytes 663556
  192.9 13.6 %all-to-all-start.12 = ((bf16[8,32,1536]{2,1,0:T(8,128)(2,1)}), bf16[8,32,1536]{2,1,0:T(8,128)(2,1)S(1)}, u32[]{:S(2)}, u32[]{:S(2)}) async-start(bf16[8,32,1536]{2,1,0:T(8,128)(2,1)} %bitcast.28), calls=%async_computation.13 | async-start | bytes 1572864 | tf_op jit(solution)/shard_map/all_to_all | solution.py:308
  197.2 1.0 copy-start.13
  206.5 45.3 %copy-start.5 = (bf16[768,768]{1,0:T(8,128)(2,1)S(1)}, bf16[768,768]{1,0:T(8,128)(2,1)}, u32[]{:S(2)}) copy-start(bf16[768,768]{1,0:T(8,128)(2,1)} %wv.5) | copy-start | bytes 3538948
  230.2 21.6 %copy-start.1 = (bf16[768,768]{1,0:T(8,128)(2,1)S(1)}, bf16[768,768]{1,0:T(8,128)(2,1)}, u32[]{:S(2)}) copy-start(bf16[768,768]{1,0:T(8,128)(2,1)} %wq.5) | copy-start | bytes 3538948
  230.2 21.6 %copy-start.3 = (bf16[768,768]{1,0:T(8,128)(2,1)S(1)}, bf16[768,768]{1,0:T(8,128)(2,1)}, u32[]{:S(2)}) copy-start(bf16[768,768]{1,0:T(8,128)(2,1)} %wk.5) | copy-start | bytes 3538948
  251.8 1.0 copy-start.11
  (3 other events, 2.1 us)
Sparse Core Ops, SparseCore 0:
  60.9 23.1 all-gather.1
  163.4 22.9 reduce-scatter.1
